TPU v7x, 256 devices: a whole 4x4x8 slice. The times are simulated.
256 devices in a mesh: tm: 16 (over y, z_lo, core), space: 16 (over x, z_hi).
Axes of the slice: x: 4, y: 4, z: 8 (z_hi: 4, z_lo: 2; z = z_hi * 2 + z_lo), core: 2. Of those that a mesh axis runs over, the one named last changes fastest.
Arguments:
- initial: float32 [2, 32, 128, 128], P(None, 'space'), may hold values from 0 to 1
- estimate: float32 [16, 2, 32, 128, 128], P('tm', None, 'space'), may hold values from 0 to 1, as said below
- feed_rate: float32 [32, 128, 128], P('space'), may hold values from 0.01 to 0.08
- kill_rate: float32 [32, 128, 128], P('space'), may hold values from 0.02 to 0.07
Outputs:
- corrected: float32 [16, 2, 32, 128, 128], P('tm', None, 'space')
- residual: float32 [16, 2, 32, 128, 128], P('tm', None, 'space')
Inputs may be any that keep to these rules, and one draw needn't show every extreme that they name: `estimate`: substrate and catalyst values.
All inputs are finite; a program needn't handle non-finite values.
Results may differ from a plain program's by a relative error of at most 0.00002.
Values sent between devices are 32-bit elements; how exact they have to be, the bound alone decides.
A program may use at most 64 MiB of HBM per device.

v0:
```python
import jax
import jax.numpy as jnp
from jax import lax
from jax.sharding import PartitionSpec as P

FACTOR = 4


time_step = 0.25
diffusion_substrate = 0.16
diffusion_catalyst = 0.08


def padded_2(block, sides, width):
    for axis, dim in sides:
        count = lax.axis_size(axis)
        forward = [(i, i + 1) for i in range(count - 1)]
        forward.append((count - 1, 0))
        backward = [(target, source) for source, target in forward]
        low = lax.ppermute(
            lax.slice_in_dim(block, block.shape[dim] - width, None, axis=dim), axis, forward
        )
        high = lax.ppermute(lax.slice_in_dim(block, 0, width, axis=dim), axis, backward)
        block = jnp.concatenate([low, block, high], axis=dim)
    return block


def shifted(array, axis, by):
    length = lax.axis_size(axis)
    pairs = [(i, i + by) for i in range(length) if 0 <= i + by < length]
    return lax.ppermute(array, axis, pairs)


def advance(extended, coefficients, step_size):
    middle = extended[..., 1:-1, :, :]
    neighbours = extended[..., 2:, :, :] + extended[..., :-2, :, :]
    neighbours = neighbours + jnp.roll(middle, 1, -2) + jnp.roll(middle, -1, -2)
    neighbours = neighbours + jnp.roll(middle, 1, -1) + jnp.roll(middle, -1, -1)
    laplace = neighbours - 6.0 * middle
    substrate = middle[..., 0, :, :, :]
    catalyst = middle[..., 1, :, :, :]
    reaction = substrate * catalyst * catalyst
    feeding = coefficients[0]
    killing = coefficients[1]
    new_substrate = substrate + step_size * (
        diffusion_substrate * laplace[..., 0, :, :, :] - reaction + feeding * (1.0 - substrate)
    )
    new_catalyst = catalyst + step_size * (
        diffusion_catalyst * laplace[..., 1, :, :, :] + reaction - (feeding + killing) * catalyst
    )
    return jnp.stack([new_substrate, new_catalyst], axis=-4)


def on_device(initial, estimate, feed_rate, kill_rate):
    coefficients = jnp.stack([feed_rate, kill_rate])
    position = lax.axis_index("tm")

    def fine_step(field):
        padded = padded_2(field, (("space", 1),), 1)
        return advance(padded, coefficients, time_step)

    def coarse_step(field):
        padded = padded_2(field, (("space", 1),), 1)
        return advance(padded, coefficients, time_step * FACTOR)

    def start_of(ends):
        received = shifted(ends, "tm", 1)
        return jnp.where(position == 0, initial, received)

    def all_fine(field):
        for count in range(FACTOR):
            field = fine_step(field)
        return field

    first = start_of(estimate[0])
    ends = all_fine(first)
    second = start_of(ends)
    fine_end = all_fine(second)
    residual = fine_end - ends
    defect = fine_end - coarse_step(second)
    turns = lax.axis_size("tm")

    def serial_turn(turn_index, coarse_value):
        received = shifted(coarse_value, "tm", 1)
        previous = jnp.where(position == 0, initial, received)
        return coarse_step(previous) + defect

    corrected = lax.fori_loop(0, turns, serial_turn, defect)
    return (corrected[None], residual[None])


def solution(mesh):
    placed = (
        P(None, "space", None, None),
        P("tm", None, "space", None, None),
        P("space", None, None),
        P("space", None, None),
    )
    return jax.shard_map(
        on_device,
        mesh=mesh,
        in_specs=placed,
        out_specs=(P("tm", None, "space", None, None), P("tm", None, "space", None, None)),
        check_vma=False,
    )
```

profile of v0, /device:TPU:22, one launch (start us, length us, event | category | flops | bytes accessed | tf_op | source)
XLA Modules:
  0.0 456.0 jit_solution(16595391685706786181)
XLA Ops:
  2.6 6.9 %collective-permute-done.3 = f32[2,2,128,128]{3,2,1,0:T(8,128)S(1)} collective-permute-done((f32[2,2,128,128]{3,2,1,0:T(8,128)}, f32[2,2,128,128]{3,2,1,0:T(8,128)S(1)}, u32[]{:S(2)}, u32[]{:S(2)}) %collective-permute-start.3) | collective-permute-done | bytes 262176 | tf_op jit(solution)/shard_map/ppermute | solution.py:31
  9.8 6.6 %collective-permute-start.4 = (f32[2,1,128,128]{3,2,1,0:T(8,128)S(1)}, f32[2,1,128,128]{3,2,1,0:T(8,128)S(1)}, u32[]{:S(2)}, u32[]{:S(2)}) collective-permute-start(f32[2,1,128,128]{3,2,1,0:T(8,128)S(1)} %get-tuple-element.214), channel_id=1, source_target_pairs={{1,0},{2,1},{3,2},{4,3},{5,4},{6,5},{7,6},{8,7},{9,8},{10,9},{11,1... | collective-permute-start | bytes 393224 | tf_op jit(solution)/shard_map/ppermute | solution.py:23
  16.5 4.7 %collective-permute-done.4 = f32[2,1,128,128]{3,2,1,0:T(8,128)S(1)} collective-permute-done((f32[2,1,128,128]{3,2,1,0:T(8,128)S(1)}, f32[2,1,128,128]{3,2,1,0:T(8,128)S(1)}, u32[]{:S(2)}, u32[]{:S(2)}) %collective-permute-start.4) | collective-permute-done | bytes 131104 | tf_op jit(solution)/shard_map/ppermute | solution.py:23
  59.1 6.7 %collective-permute-done.12 = f32[2,2,128,128]{3,2,1,0:T(8,128)S(1)} collective-permute-done((f32[2,2,128,128]{3,2,1,0:T(8,128)S(1)}, f32[2,2,128,128]{3,2,1,0:T(8,128)S(1)}, u32[]{:S(2)}, u32[]{:S(2)}) %collective-permute-start.12) | collective-permute-done | bytes 262176 | tf_op jit(solution)/shard_map/ppermute | solution.py:31
  72.5 4.5 collective-permute-done.14
  80.7 6.6 %collective-permute-done.15 = f32[2,1,128,128]{3,2,1,0:T(8,128)S(1)} collective-permute-done((f32[2,1,128,128]{3,2,1,0:T(8,128)S(1)}, f32[2,1,128,128]{3,2,1,0:T(8,128)S(1)}, u32[]{:S(2)}, u32[]{:S(2)}) %collective-permute-start.15) | collective-permute-done | bytes 131104 | tf_op jit(solution)/shard_map/ppermute | solution.py:23
  93.4 4.8 %collective-permute-done.17 = f32[2,1,128,128]{3,2,1,0:T(8,128)S(1)} collective-permute-done((f32[2,1,128,128]{3,2,1,0:T(8,128)S(1)}, f32[2,1,128,128]{3,2,1,0:T(8,128)S(1)}, u32[]{:S(2)}, u32[]{:S(2)}) %collective-permute-start.17) | collective-permute-done | bytes 131104 | tf_op jit(solution)/shard_map/ppermute | solution.py:23
  111.7 343.6 %while.12 = (s32[]{:T(128)}, f32[2,2,128,128]{3,2,1,0:T(8,128)S(1)}, pred[]{:T(512)}, f32[2,2,128,128]{3,2,1,0:T(8,128)S(1)}, f32[2,128,128]{2,1,0:T(8,128)S(1)}...) while((s32[]{:T(128)}, f32[2,2,128,128]{3,2,1,0:T(8,128)S(1)}, pred[]{:T(512)}, ...), condition=%wide.region_1.2_spmd, body=%wide.region_0.1_spmd.sunk | while | flops 1474562 | bytes 9175246 | solution.py:88
  113.6 6.7 %collective-permute-done = f32[2,2,128,128]{3,2,1,0:T(8,128)S(1)} collective-permute-done((f32[2,2,128,128]{3,2,1,0:T(8,128)S(1)}, f32[2,2,128,128]{3,2,1,0:T(8,128)S(1)}, u32[]{:S(2)}, u32[]{:S(2)}) %collective-permute-start) | collective-permute-done | bytes 262176 | tf_op jit(solution)/shard_map/while/body/eval_jaxpr/ppermute | solution.py:31
  131.4 6.7 %collective-permute-done = f32[2,2,128,128]{3,2,1,0:T(8,128)S(1)} collective-permute-done((f32[2,2,128,128]{3,2,1,0:T(8,128)S(1)}, f32[2,2,128,128]{3,2,1,0:T(8,128)S(1)}, u32[]{:S(2)}, u32[]{:S(2)}) %collective-permute-start) | collective-permute-done | bytes 262176 | tf_op jit(solution)/shard_map/while/body/eval_jaxpr/ppermute | solution.py:31
  151.7 6.7 %collective-permute-done = f32[2,2,128,128]{3,2,1,0:T(8,128)S(1)} collective-permute-done((f32[2,2,128,128]{3,2,1,0:T(8,128)S(1)}, f32[2,2,128,128]{3,2,1,0:T(8,128)S(1)}, u32[]{:S(2)}, u32[]{:S(2)}) %collective-permute-start) | collective-permute-done | bytes 262176 | tf_op jit(solution)/shard_map/while/body/eval_jaxpr/ppermute | solution.py:31
  158.7 9.5 %collective-permute-start.1 = (f32[2,1,128,128]{3,2,1,0:T(8,128)S(1)}, f32[2,1,128,128]{3,2,1,0:T(8,128)S(1)}, u32[]{:S(2)}, u32[]{:S(2)}) collective-permute-start(f32[2,1,128,128]{3,2,1,0:T(8,128)S(1)} %get-tuple-element.271), channel_id=1, source_target_pairs={{0,1},{1,2},{2,3},{3,4},{4,5},{5,6},{6,7},{7,8},{8,9},{9,10},{10,1... | collective-permute-start | bytes 393224 | tf_op jit(solution)/shard_map/while/body/eval_jaxpr/ppermute | solution.py:20
  176.7 6.7 %collective-permute-done = f32[2,2,128,128]{3,2,1,0:T(8,128)S(1)} collective-permute-done((f32[2,2,128,128]{3,2,1,0:T(8,128)S(1)}, f32[2,2,128,128]{3,2,1,0:T(8,128)S(1)}, u32[]{:S(2)}, u32[]{:S(2)}) %collective-permute-start) | collective-permute-done | bytes 262176 | tf_op jit(solution)/shard_map/while/body/eval_jaxpr/ppermute | solution.py:31
  183.8 5.0 %collective-permute-start.1 = (f32[2,1,128,128]{3,2,1,0:T(8,128)S(1)}, f32[2,1,128,128]{3,2,1,0:T(8,128)S(1)}, u32[]{:S(2)}, u32[]{:S(2)}) collective-permute-start(f32[2,1,128,128]{3,2,1,0:T(8,128)S(1)} %get-tuple-element.271), channel_id=1, source_target_pairs={{0,1},{1,2},{2,3},{3,4},{4,5},{5,6},{6,7},{7,8},{8,9},{9,10},{10,1... | collective-permute-start | bytes 393224 | tf_op jit(solution)/shard_map/while/body/eval_jaxpr/ppermute | solution.py:20
  196.9 6.7 %collective-permute-done = f32[2,2,128,128]{3,2,1,0:T(8,128)S(1)} collective-permute-done((f32[2,2,128,128]{3,2,1,0:T(8,128)S(1)}, f32[2,2,128,128]{3,2,1,0:T(8,128)S(1)}, u32[]{:S(2)}, u32[]{:S(2)}) %collective-permute-start) | collective-permute-done | bytes 262176 | tf_op jit(solution)/shard_map/while/body/eval_jaxpr/ppermute | solution.py:31
  203.9 5.9 %collective-permute-start.1 = (f32[2,1,128,128]{3,2,1,0:T(8,128)S(1)}, f32[2,1,128,128]{3,2,1,0:T(8,128)S(1)}, u32[]{:S(2)}, u32[]{:S(2)}) collective-permute-start(f32[2,1,128,128]{3,2,1,0:T(8,128)S(1)} %get-tuple-element.271), channel_id=1, source_target_pairs={{0,1},{1,2},{2,3},{3,4},{4,5},{5,6},{6,7},{7,8},{8,9},{9,10},{10,1... | collective-permute-start | bytes 393224 | tf_op jit(solution)/shard_map/while/body/eval_jaxpr/ppermute | solution.py:20
  218.7 6.7 %collective-permute-done = f32[2,2,128,128]{3,2,1,0:T(8,128)S(1)} collective-permute-done((f32[2,2,128,128]{3,2,1,0:T(8,128)S(1)}, f32[2,2,128,128]{3,2,1,0:T(8,128)S(1)}, u32[]{:S(2)}, u32[]{:S(2)}) %collective-permute-start) | collective-permute-done | bytes 262176 | tf_op jit(solution)/shard_map/while/body/eval_jaxpr/ppermute | solution.py:31
  225.7 8.6 %collective-permute-start.1 = (f32[2,1,128,128]{3,2,1,0:T(8,128)S(1)}, f32[2,1,128,128]{3,2,1,0:T(8,128)S(1)}, u32[]{:S(2)}, u32[]{:S(2)}) collective-permute-start(f32[2,1,128,128]{3,2,1,0:T(8,128)S(1)} %get-tuple-element.271), channel_id=1, source_target_pairs={{0,1},{1,2},{2,3},{3,4},{4,5},{5,6},{6,7},{7,8},{8,9},{9,10},{10,1... | collective-permute-start | bytes 393224 | tf_op jit(solution)/shard_map/while/body/eval_jaxpr/ppermute | solution.py:20
  242.9 8.1 %collective-permute-done = f32[2,2,128,128]{3,2,1,0:T(8,128)S(1)} collective-permute-done((f32[2,2,128,128]{3,2,1,0:T(8,128)S(1)}, f32[2,2,128,128]{3,2,1,0:T(8,128)S(1)}, u32[]{:S(2)}, u32[]{:S(2)}) %collective-permute-start) | collective-permute-done | bytes 262176 | tf_op jit(solution)/shard_map/while/body/eval_jaxpr/ppermute | solution.py:31
  263.8 6.7 %collective-permute-done = f32[2,2,128,128]{3,2,1,0:T(8,128)S(1)} collective-permute-done((f32[2,2,128,128]{3,2,1,0:T(8,128)S(1)}, f32[2,2,128,128]{3,2,1,0:T(8,128)S(1)}, u32[]{:S(2)}, u32[]{:S(2)}) %collective-permute-start) | collective-permute-done | bytes 262176 | tf_op jit(solution)/shard_map/while/body/eval_jaxpr/ppermute | solution.py:31
  270.8 5.1 %collective-permute-start.1 = (f32[2,1,128,128]{3,2,1,0:T(8,128)S(1)}, f32[2,1,128,128]{3,2,1,0:T(8,128)S(1)}, u32[]{:S(2)}, u32[]{:S(2)}) collective-permute-start(f32[2,1,128,128]{3,2,1,0:T(8,128)S(1)} %get-tuple-element.271), channel_id=1, source_target_pairs={{0,1},{1,2},{2,3},{3,4},{4,5},{5,6},{6,7},{7,8},{8,9},{9,10},{10,1... | collective-permute-start | bytes 393224 | tf_op jit(solution)/shard_map/while/body/eval_jaxpr/ppermute | solution.py:20
  284.1 8.9 %collective-permute-done = f32[2,2,128,128]{3,2,1,0:T(8,128)S(1)} collective-permute-done((f32[2,2,128,128]{3,2,1,0:T(8,128)S(1)}, f32[2,2,128,128]{3,2,1,0:T(8,128)S(1)}, u32[]{:S(2)}, u32[]{:S(2)}) %collective-permute-start) | collective-permute-done | bytes 262176 | tf_op jit(solution)/shard_map/while/body/eval_jaxpr/ppermute | solution.py:31
  293.4 7.2 %collective-permute-start.1 = (f32[2,1,128,128]{3,2,1,0:T(8,128)S(1)}, f32[2,1,128,128]{3,2,1,0:T(8,128)S(1)}, u32[]{:S(2)}, u32[]{:S(2)}) collective-permute-start(f32[2,1,128,128]{3,2,1,0:T(8,128)S(1)} %get-tuple-element.271), channel_id=1, source_target_pairs={{0,1},{1,2},{2,3},{3,4},{4,5},{5,6},{6,7},{7,8},{8,9},{9,10},{10,1... | collective-permute-start | bytes 393224 | tf_op jit(solution)/shard_map/while/body/eval_jaxpr/ppermute | solution.py:20
  308.7 9.5 %collective-permute-done = f32[2,2,128,128]{3,2,1,0:T(8,128)S(1)} collective-permute-done((f32[2,2,128,128]{3,2,1,0:T(8,128)S(1)}, f32[2,2,128,128]{3,2,1,0:T(8,128)S(1)}, u32[]{:S(2)}, u32[]{:S(2)}) %collective-permute-start) | collective-permute-done | bytes 262176 | tf_op jit(solution)/shard_map/while/body/eval_jaxpr/ppermute | solution.py:31
  329.8 6.9 %collective-permute-done = f32[2,2,128,128]{3,2,1,0:T(8,128)S(1)} collective-permute-done((f32[2,2,128,128]{3,2,1,0:T(8,128)S(1)}, f32[2,2,128,128]{3,2,1,0:T(8,128)S(1)}, u32[]{:S(2)}, u32[]{:S(2)}) %collective-permute-start) | collective-permute-done | bytes 262176 | tf_op jit(solution)/shard_map/while/body/eval_jaxpr/ppermute | solution.py:31
  349.2 8.8 %collective-permute-done = f32[2,2,128,128]{3,2,1,0:T(8,128)S(1)} collective-permute-done((f32[2,2,128,128]{3,2,1,0:T(8,128)S(1)}, f32[2,2,128,128]{3,2,1,0:T(8,128)S(1)}, u32[]{:S(2)}, u32[]{:S(2)}) %collective-permute-start) | collective-permute-done | bytes 262176 | tf_op jit(solution)/shard_map/while/body/eval_jaxpr/ppermute | solution.py:31
  370.6 8.8 %collective-permute-done = f32[2,2,128,128]{3,2,1,0:T(8,128)S(1)} collective-permute-done((f32[2,2,128,128]{3,2,1,0:T(8,128)S(1)}, f32[2,2,128,128]{3,2,1,0:T(8,128)S(1)}, u32[]{:S(2)}, u32[]{:S(2)}) %collective-permute-start) | collective-permute-done | bytes 262176 | tf_op jit(solution)/shard_map/while/body/eval_jaxpr/ppermute | solution.py:31
  379.8 5.6 %collective-permute-start.1 = (f32[2,1,128,128]{3,2,1,0:T(8,128)S(1)}, f32[2,1,128,128]{3,2,1,0:T(8,128)S(1)}, u32[]{:S(2)}, u32[]{:S(2)}) collective-permute-start(f32[2,1,128,128]{3,2,1,0:T(8,128)S(1)} %get-tuple-element.271), channel_id=1, source_target_pairs={{0,1},{1,2},{2,3},{3,4},{4,5},{5,6},{6,7},{7,8},{8,9},{9,10},{10,1... | collective-permute-start | bytes 393224 | tf_op jit(solution)/shard_map/while/body/eval_jaxpr/ppermute | solution.py:20
  393.6 7.4 %collective-permute-done = f32[2,2,128,128]{3,2,1,0:T(8,128)S(1)} collective-permute-done((f32[2,2,128,128]{3,2,1,0:T(8,128)S(1)}, f32[2,2,128,128]{3,2,1,0:T(8,128)S(1)}, u32[]{:S(2)}, u32[]{:S(2)}) %collective-permute-start) | collective-permute-done | bytes 262176 | tf_op jit(solution)/shard_map/while/body/eval_jaxpr/ppermute | solution.py:31
  401.4 5.5 %collective-permute-start.1 = (f32[2,1,128,128]{3,2,1,0:T(8,128)S(1)}, f32[2,1,128,128]{3,2,1,0:T(8,128)S(1)}, u32[]{:S(2)}, u32[]{:S(2)}) collective-permute-start(f32[2,1,128,128]{3,2,1,0:T(8,128)S(1)} %get-tuple-element.271), channel_id=1, source_target_pairs={{0,1},{1,2},{2,3},{3,4},{4,5},{5,6},{6,7},{7,8},{8,9},{9,10},{10,1... | collective-permute-start | bytes 393224 | tf_op jit(solution)/shard_map/while/body/eval_jaxpr/ppermute | solution.py:20
  415.1 9.5 %collective-permute-done = f32[2,2,128,128]{3,2,1,0:T(8,128)S(1)} collective-permute-done((f32[2,2,128,128]{3,2,1,0:T(8,128)S(1)}, f32[2,2,128,128]{3,2,1,0:T(8,128)S(1)}, u32[]{:S(2)}, u32[]{:S(2)}) %collective-permute-start) | collective-permute-done | bytes 262176 | tf_op jit(solution)/shard_map/while/body/eval_jaxpr/ppermute | solution.py:31
  436.5 9.5 %collective-permute-done = f32[2,2,128,128]{3,2,1,0:T(8,128)S(1)} collective-permute-done((f32[2,2,128,128]{3,2,1,0:T(8,128)S(1)}, f32[2,2,128,128]{3,2,1,0:T(8,128)S(1)}, u32[]{:S(2)}, u32[]{:S(2)}) %collective-permute-start) | collective-permute-done | bytes 262176 | tf_op jit(solution)/shard_map/while/body/eval_jaxpr/ppermute | solution.py:31
  (316 shorter events, 236.4 us)
Async XLA Ops:
  0.6 8.8 %collective-permute-start.3 = (f32[2,2,128,128]{3,2,1,0:T(8,128)}, f32[2,2,128,128]{3,2,1,0:T(8,128)S(1)}, u32[]{:S(2)}, u32[]{:S(2)}) collective-permute-start(f32[2,2,128,128]{3,2,1,0:T(8,128)} %bitcast.315), channel_id=1, source_target_pairs={{0,16},{16,32},{32,48},{48,64},{64,80},{80,96},{96,112},{112,128},... | collective-permute-start | bytes 786440 | tf_op jit(solution)/shard_map/ppermute | solution.py:31
  9.8 11.4 %collective-permute-start.4 = (f32[2,1,128,128]{3,2,1,0:T(8,128)S(1)}, f32[2,1,128,128]{3,2,1,0:T(8,128)S(1)}, u32[]{:S(2)}, u32[]{:S(2)}) collective-permute-start(f32[2,1,128,128]{3,2,1,0:T(8,128)S(1)} %get-tuple-element.214), channel_id=1, source_target_pairs={{1,0},{2,1},{3,2},{4,3},{5,4},{6,5},{7,6},{8,7},{9,8},{10,9},{11,1... | collective-permute-start | bytes 393224 | tf_op jit(solution)/shard_map/ppermute | solution.py:23
  16.5 8.8 %collective-permute-start.5 = (f32[2,1,128,128]{3,2,1,0:T(8,128)S(1)}, f32[2,1,128,128]{3,2,1,0:T(8,128)S(1)}, u32[]{:S(2)}, u32[]{:S(2)}) collective-permute-start(f32[2,1,128,128]{3,2,1,0:T(8,128)S(1)} %get-tuple-element.215), channel_id=1, source_target_pairs={{0,1},{1,2},{2,3},{3,4},{4,5},{5,6},{6,7},{7,8},{8,9},{9,10},{10,1... | collective-permute-start | bytes 393224 | tf_op jit(solution)/shard_map/ppermute | solution.py:20
  37.1 9.4 %collective-permute-start.9 = (f32[2,1,128,128]{3,2,1,0:T(8,128)S(1)}, f32[2,1,128,128]{3,2,1,0:T(8,128)S(1)}, u32[]{:S(2)}, u32[]{:S(2)}) collective-permute-start(f32[2,1,128,128]{3,2,1,0:T(8,128)S(1)} %get-tuple-element.195), channel_id=1, source_target_pairs={{0,1},{1,2},{2,3},{3,4},{4,5},{5,6},{6,7},{7,8},{8,9},{9,10},{10,1... | collective-permute-start | bytes 393224 | tf_op jit(solution)/shard_map/ppermute | solution.py:20
  47.2 9.5 %collective-permute-start.11 = (f32[2,1,128,128]{3,2,1,0:T(8,128)S(1)}, f32[2,1,128,128]{3,2,1,0:T(8,128)S(1)}, u32[]{:S(2)}, u32[]{:S(2)}) collective-permute-start(f32[2,1,128,128]{3,2,1,0:T(8,128)S(1)} %get-tuple-element.185), channel_id=1, source_target_pairs={{0,1},{1,2},{2,3},{3,4},{4,5},{5,6},{6,7},{7,8},{8,9},{9,10},{10,1... | collective-permute-start | bytes 393224 | tf_op jit(solution)/shard_map/ppermute | solution.py:20
  57.0 8.7 %collective-permute-start.12 = (f32[2,2,128,128]{3,2,1,0:T(8,128)S(1)}, f32[2,2,128,128]{3,2,1,0:T(8,128)S(1)}, u32[]{:S(2)}, u32[]{:S(2)}) collective-permute-start(f32[2,2,128,128]{3,2,1,0:T(8,128)S(1)} %pad_maximum_fusion.36), channel_id=1, source_target_pairs={{0,16},{16,32},{32,48},{48,64},{64,80},{80,96},{96,112},{112,128},... | collective-permute-start | bytes 786440 | tf_op jit(solution)/shard_map/ppermute | solution.py:31
  66.2 10.8 %collective-permute-start.14 = (f32[2,1,128,128]{3,2,1,0:T(8,128)S(1)}, f32[2,1,128,128]{3,2,1,0:T(8,128)S(1)}, u32[]{:S(2)}, u32[]{:S(2)}) collective-permute-start(f32[2,1,128,128]{3,2,1,0:T(8,128)S(1)} %get-tuple-element.175), channel_id=1, source_target_pairs={{0,1},{1,2},{2,3},{3,4},{4,5},{5,6},{6,7},{7,8},{8,9},{9,10},{10,1... | collective-permute-start | bytes 393224 | tf_op jit(solution)/shard_map/ppermute | solution.py:20
  77.6 9.7 %collective-permute-start.15 = (f32[2,1,128,128]{3,2,1,0:T(8,128)S(1)}, f32[2,1,128,128]{3,2,1,0:T(8,128)S(1)}, u32[]{:S(2)}, u32[]{:S(2)}) collective-permute-start(f32[2,1,128,128]{3,2,1,0:T(8,128)S(1)} %get-tuple-element.164), channel_id=1, source_target_pairs={{1,0},{2,1},{3,2},{4,3},{5,4},{6,5},{7,6},{8,7},{9,8},{10,9},{11,1... | collective-permute-start | bytes 393224 | tf_op jit(solution)/shard_map/ppermute | solution.py:23
  77.7 12.0 %collective-permute-start.16 = (f32[2,1,128,128]{3,2,1,0:T(8,128)S(1)}, f32[2,1,128,128]{3,2,1,0:T(8,128)S(1)}, u32[]{:S(2)}, u32[]{:S(2)}) collective-permute-start(f32[2,1,128,128]{3,2,1,0:T(8,128)S(1)} %get-tuple-element.165), channel_id=1, source_target_pairs={{0,1},{1,2},{2,3},{3,4},{4,5},{5,6},{6,7},{7,8},{8,9},{9,10},{10,1... | collective-permute-start | bytes 393224 | tf_op jit(solution)/shard_map/ppermute | solution.py:20
  90.5 11.4 %collective-permute-start.18 = (f32[2,1,128,128]{3,2,1,0:T(8,128)S(1)}, f32[2,1,128,128]{3,2,1,0:T(8,128)S(1)}, u32[]{:S(2)}, u32[]{:S(2)}) collective-permute-start(f32[2,1,128,128]{3,2,1,0:T(8,128)S(1)} %get-tuple-element.155), channel_id=1, source_target_pairs={{0,1},{1,2},{2,3},{3,4},{4,5},{5,6},{6,7},{7,8},{8,9},{9,10},{10,1... | collective-permute-start | bytes 393224 | tf_op jit(solution)/shard_map/ppermute | solution.py:20
  129.5 8.6 %collective-permute-start = (f32[2,2,128,128]{3,2,1,0:T(8,128)S(1)}, f32[2,2,128,128]{3,2,1,0:T(8,128)S(1)}, u32[]{:S(2)}, u32[]{:S(2)}) collective-permute-start(f32[2,2,128,128]{3,2,1,0:T(8,128)S(1)} %get-tuple-element.292), channel_id=1, source_target_pairs={{0,16},{16,32},{32,48},{48,64},{64,80},{80,96},{96,112},{112,128},... | collective-permute-start | bytes 786440 | tf_op jit(solution)/shard_map/while/body/eval_jaxpr/ppermute | solution.py:31
  138.5 9.5 %collective-permute-start.1 = (f32[2,1,128,128]{3,2,1,0:T(8,128)S(1)}, f32[2,1,128,128]{3,2,1,0:T(8,128)S(1)}, u32[]{:S(2)}, u32[]{:S(2)}) collective-permute-start(f32[2,1,128,128]{3,2,1,0:T(8,128)S(1)} %get-tuple-element.271), channel_id=1, source_target_pairs={{0,1},{1,2},{2,3},{3,4},{4,5},{5,6},{6,7},{7,8},{8,9},{9,10},{10,1... | collective-permute-start | bytes 393224 | tf_op jit(solution)/shard_map/while/body/eval_jaxpr/ppermute | solution.py:20
  139.7 9.7 %collective-permute-start.2 = (f32[2,1,128,128]{3,2,1,0:T(8,128)S(1)}, f32[2,1,128,128]{3,2,1,0:T(8,128)S(1)}, u32[]{:S(2)}, u32[]{:S(2)}) collective-permute-start(f32[2,1,128,128]{3,2,1,0:T(8,128)S(1)} %get-tuple-element.272), channel_id=1, source_target_pairs={{1,0},{2,1},{3,2},{4,3},{5,4},{6,5},{7,6},{8,7},{9,8},{10,9},{11,1... | collective-permute-start | bytes 393224 | tf_op jit(solution)/shard_map/while/body/eval_jaxpr/ppermute | solution.py:23
  149.7 8.6 %collective-permute-start = (f32[2,2,128,128]{3,2,1,0:T(8,128)S(1)}, f32[2,2,128,128]{3,2,1,0:T(8,128)S(1)}, u32[]{:S(2)}, u32[]{:S(2)}) collective-permute-start(f32[2,2,128,128]{3,2,1,0:T(8,128)S(1)} %get-tuple-element.292), channel_id=1, source_target_pairs={{0,16},{16,32},{32,48},{48,64},{64,80},{80,96},{96,112},{112,128},... | collective-permute-start | bytes 786440 | tf_op jit(solution)/shard_map/while/body/eval_jaxpr/ppermute | solution.py:31
  158.7 12.0 %collective-permute-start.1 = (f32[2,1,128,128]{3,2,1,0:T(8,128)S(1)}, f32[2,1,128,128]{3,2,1,0:T(8,128)S(1)}, u32[]{:S(2)}, u32[]{:S(2)}) collective-permute-start(f32[2,1,128,128]{3,2,1,0:T(8,128)S(1)} %get-tuple-element.271), channel_id=1, source_target_pairs={{0,1},{1,2},{2,3},{3,4},{4,5},{5,6},{6,7},{7,8},{8,9},{9,10},{10,1... | collective-permute-start | bytes 393224 | tf_op jit(solution)/shard_map/while/body/eval_jaxpr/ppermute | solution.py:20
  174.8 8.6 %collective-permute-start = (f32[2,2,128,128]{3,2,1,0:T(8,128)S(1)}, f32[2,2,128,128]{3,2,1,0:T(8,128)S(1)}, u32[]{:S(2)}, u32[]{:S(2)}) collective-permute-start(f32[2,2,128,128]{3,2,1,0:T(8,128)S(1)} %get-tuple-element.292), channel_id=1, source_target_pairs={{0,16},{16,32},{32,48},{48,64},{64,80},{80,96},{96,112},{112,128},... | collective-permute-start | bytes 786440 | tf_op jit(solution)/shard_map/while/body/eval_jaxpr/ppermute | solution.py:31
  195.0 8.6 %collective-permute-start = (f32[2,2,128,128]{3,2,1,0:T(8,128)S(1)}, f32[2,2,128,128]{3,2,1,0:T(8,128)S(1)}, u32[]{:S(2)}, u32[]{:S(2)}) collective-permute-start(f32[2,2,128,128]{3,2,1,0:T(8,128)S(1)} %get-tuple-element.292), channel_id=1, source_target_pairs={{0,16},{16,32},{32,48},{48,64},{64,80},{80,96},{96,112},{112,128},... | collective-permute-start | bytes 786440 | tf_op jit(solution)/shard_map/while/body/eval_jaxpr/ppermute | solution.py:31
  203.9 8.6 %collective-permute-start.1 = (f32[2,1,128,128]{3,2,1,0:T(8,128)S(1)}, f32[2,1,128,128]{3,2,1,0:T(8,128)S(1)}, u32[]{:S(2)}, u32[]{:S(2)}) collective-permute-start(f32[2,1,128,128]{3,2,1,0:T(8,128)S(1)} %get-tuple-element.271), channel_id=1, source_target_pairs={{0,1},{1,2},{2,3},{3,4},{4,5},{5,6},{6,7},{7,8},{8,9},{9,10},{10,1... | collective-permute-start | bytes 393224 | tf_op jit(solution)/shard_map/while/body/eval_jaxpr/ppermute | solution.py:20
  216.7 8.6 %collective-permute-start = (f32[2,2,128,128]{3,2,1,0:T(8,128)S(1)}, f32[2,2,128,128]{3,2,1,0:T(8,128)S(1)}, u32[]{:S(2)}, u32[]{:S(2)}) collective-permute-start(f32[2,2,128,128]{3,2,1,0:T(8,128)S(1)} %get-tuple-element.292), channel_id=1, source_target_pairs={{0,16},{16,32},{32,48},{48,64},{64,80},{80,96},{96,112},{112,128},... | collective-permute-start | bytes 786440 | tf_op jit(solution)/shard_map/while/body/eval_jaxpr/ppermute | solution.py:31
  225.7 12.3 %collective-permute-start.1 = (f32[2,1,128,128]{3,2,1,0:T(8,128)S(1)}, f32[2,1,128,128]{3,2,1,0:T(8,128)S(1)}, u32[]{:S(2)}, u32[]{:S(2)}) collective-permute-start(f32[2,1,128,128]{3,2,1,0:T(8,128)S(1)} %get-tuple-element.271), channel_id=1, source_target_pairs={{0,1},{1,2},{2,3},{3,4},{4,5},{5,6},{6,7},{7,8},{8,9},{9,10},{10,1... | collective-permute-start | bytes 393224 | tf_op jit(solution)/shard_map/while/body/eval_jaxpr/ppermute | solution.py:20
  241.0 10.0 %collective-permute-start = (f32[2,2,128,128]{3,2,1,0:T(8,128)S(1)}, f32[2,2,128,128]{3,2,1,0:T(8,128)S(1)}, u32[]{:S(2)}, u32[]{:S(2)}) collective-permute-start(f32[2,2,128,128]{3,2,1,0:T(8,128)S(1)} %get-tuple-element.292), channel_id=1, source_target_pairs={{0,16},{16,32},{32,48},{48,64},{64,80},{80,96},{96,112},{112,128},... | collective-permute-start | bytes 786440 | tf_op jit(solution)/shard_map/while/body/eval_jaxpr/ppermute | solution.py:31
  261.9 8.6 %collective-permute-start = (f32[2,2,128,128]{3,2,1,0:T(8,128)S(1)}, f32[2,2,128,128]{3,2,1,0:T(8,128)S(1)}, u32[]{:S(2)}, u32[]{:S(2)}) collective-permute-start(f32[2,2,128,128]{3,2,1,0:T(8,128)S(1)} %get-tuple-element.292), channel_id=1, source_target_pairs={{0,16},{16,32},{32,48},{48,64},{64,80},{80,96},{96,112},{112,128},... | collective-permute-start | bytes 786440 | tf_op jit(solution)/shard_map/while/body/eval_jaxpr/ppermute | solution.py:31
  270.8 9.0 %collective-permute-start.1 = (f32[2,1,128,128]{3,2,1,0:T(8,128)S(1)}, f32[2,1,128,128]{3,2,1,0:T(8,128)S(1)}, u32[]{:S(2)}, u32[]{:S(2)}) collective-permute-start(f32[2,1,128,128]{3,2,1,0:T(8,128)S(1)} %get-tuple-element.271), channel_id=1, source_target_pairs={{0,1},{1,2},{2,3},{3,4},{4,5},{5,6},{6,7},{7,8},{8,9},{9,10},{10,1... | collective-permute-start | bytes 393224 | tf_op jit(solution)/shard_map/while/body/eval_jaxpr/ppermute | solution.py:20
  282.2 10.9 %collective-permute-start = (f32[2,2,128,128]{3,2,1,0:T(8,128)S(1)}, f32[2,2,128,128]{3,2,1,0:T(8,128)S(1)}, u32[]{:S(2)}, u32[]{:S(2)}) collective-permute-start(f32[2,2,128,128]{3,2,1,0:T(8,128)S(1)} %get-tuple-element.292), channel_id=1, source_target_pairs={{0,16},{16,32},{32,48},{48,64},{64,80},{80,96},{96,112},{112,128},... | collective-permute-start | bytes 786440 | tf_op jit(solution)/shard_map/while/body/eval_jaxpr/ppermute | solution.py:31
  293.4 9.7 %collective-permute-start.1 = (f32[2,1,128,128]{3,2,1,0:T(8,128)S(1)}, f32[2,1,128,128]{3,2,1,0:T(8,128)S(1)}, u32[]{:S(2)}, u32[]{:S(2)}) collective-permute-start(f32[2,1,128,128]{3,2,1,0:T(8,128)S(1)} %get-tuple-element.271), channel_id=1, source_target_pairs={{0,1},{1,2},{2,3},{3,4},{4,5},{5,6},{6,7},{7,8},{8,9},{9,10},{10,1... | collective-permute-start | bytes 393224 | tf_op jit(solution)/shard_map/while/body/eval_jaxpr/ppermute | solution.py:20
  306.8 11.4 %collective-permute-start = (f32[2,2,128,128]{3,2,1,0:T(8,128)S(1)}, f32[2,2,128,128]{3,2,1,0:T(8,128)S(1)}, u32[]{:S(2)}, u32[]{:S(2)}) collective-permute-start(f32[2,2,128,128]{3,2,1,0:T(8,128)S(1)} %get-tuple-element.292), channel_id=1, source_target_pairs={{0,16},{16,32},{32,48},{48,64},{64,80},{80,96},{96,112},{112,128},... | collective-permute-start | bytes 786440 | tf_op jit(solution)/shard_map/while/body/eval_jaxpr/ppermute | solution.py:31
  327.9 8.8 %collective-permute-start = (f32[2,2,128,128]{3,2,1,0:T(8,128)S(1)}, f32[2,2,128,128]{3,2,1,0:T(8,128)S(1)}, u32[]{:S(2)}, u32[]{:S(2)}) collective-permute-start(f32[2,2,128,128]{3,2,1,0:T(8,128)S(1)} %get-tuple-element.292), channel_id=1, source_target_pairs={{0,16},{16,32},{32,48},{48,64},{64,80},{80,96},{96,112},{112,128},... | collective-permute-start | bytes 786440 | tf_op jit(solution)/shard_map/while/body/eval_jaxpr/ppermute | solution.py:31
  347.3 10.7 %collective-permute-start = (f32[2,2,128,128]{3,2,1,0:T(8,128)S(1)}, f32[2,2,128,128]{3,2,1,0:T(8,128)S(1)}, u32[]{:S(2)}, u32[]{:S(2)}) collective-permute-start(f32[2,2,128,128]{3,2,1,0:T(8,128)S(1)} %get-tuple-element.292), channel_id=1, source_target_pairs={{0,16},{16,32},{32,48},{48,64},{64,80},{80,96},{96,112},{112,128},... | collective-permute-start | bytes 786440 | tf_op jit(solution)/shard_map/while/body/eval_jaxpr/ppermute | solution.py:31
  368.7 10.8 %collective-permute-start = (f32[2,2,128,128]{3,2,1,0:T(8,128)S(1)}, f32[2,2,128,128]{3,2,1,0:T(8,128)S(1)}, u32[]{:S(2)}, u32[]{:S(2)}) collective-permute-start(f32[2,2,128,128]{3,2,1,0:T(8,128)S(1)} %get-tuple-element.292), channel_id=1, source_target_pairs={{0,16},{16,32},{32,48},{48,64},{64,80},{80,96},{96,112},{112,128},... | collective-permute-start | bytes 786440 | tf_op jit(solution)/shard_map/while/body/eval_jaxpr/ppermute | solution.py:31
  391.7 9.4 %collective-permute-start = (f32[2,2,128,128]{3,2,1,0:T(8,128)S(1)}, f32[2,2,128,128]{3,2,1,0:T(8,128)S(1)}, u32[]{:S(2)}, u32[]{:S(2)}) collective-permute-start(f32[2,2,128,128]{3,2,1,0:T(8,128)S(1)} %get-tuple-element.292), channel_id=1, source_target_pairs={{0,16},{16,32},{32,48},{48,64},{64,80},{80,96},{96,112},{112,128},... | collective-permute-start | bytes 786440 | tf_op jit(solution)/shard_map/while/body/eval_jaxpr/ppermute | solution.py:31
  413.1 11.4 %collective-permute-start = (f32[2,2,128,128]{3,2,1,0:T(8,128)S(1)}, f32[2,2,128,128]{3,2,1,0:T(8,128)S(1)}, u32[]{:S(2)}, u32[]{:S(2)}) collective-permute-start(f32[2,2,128,128]{3,2,1,0:T(8,128)S(1)} %get-tuple-element.292), channel_id=1, source_target_pairs={{0,16},{16,32},{32,48},{48,64},{64,80},{80,96},{96,112},{112,128},... | collective-permute-start | bytes 786440 | tf_op jit(solution)/shard_map/while/body/eval_jaxpr/ppermute | solution.py:31
  434.5 11.5 %collective-permute-start = (f32[2,2,128,128]{3,2,1,0:T(8,128)S(1)}, f32[2,2,128,128]{3,2,1,0:T(8,128)S(1)}, u32[]{:S(2)}, u32[]{:S(2)}) collective-permute-start(f32[2,2,128,128]{3,2,1,0:T(8,128)S(1)} %get-tuple-element.292), channel_id=1, source_target_pairs={{0,16},{16,32},{32,48},{48,64},{64,80},{80,96},{96,112},{112,128},... | collective-permute-start | bytes 786440 | tf_op jit(solution)/shard_map/while/body/eval_jaxpr/ppermute | solution.py:31
  (38 other events, 249.3 us)
where the time goes:
time: 457 us; the launch traced here: 456 us
  waiting for transfers between devices  279 us (61%)
  starting transfers between devices  157 us (34%)
  other arithmetic  10.8 us (2%)
  local copies, waits for them, and re-layouts  7.29 us (2%)
    ppermute x18, waiting for transfers between devices, shifted(): return lax.ppermute(array, axis, pairs)  138 us
    ppermute x24, starting transfers between devices, padded_2(): lax.ppermute(lax.slice_in_dim(block, block.shape[dim] - width, None, axis...  94.5 us
    ppermute x24, waiting for transfers between devices, padded_2(): lax.ppermute(lax.slice_in_dim(block, block.shape[dim] - width, None, axis...  72.5 us
    ppermute x24, waiting for transfers between devices, padded_2(): lax.ppermute(lax.slice_in_dim(block, 0, width, axis=dim), axis, backward)  68.8 us
    ppermute x18, starting transfers between devices, shifted(): return lax.ppermute(array, axis, pairs)  34.7 us
    ppermute x24, starting transfers between devices, padded_2(): lax.ppermute(lax.slice_in_dim(block, 0, width, axis=dim), axis, backward)  27.6 us
  transfers between devices with their start and end apart: 66, of which 66 were waited for; matrix products, arithmetic and copies ran while one was open for 0% of the time, Pallas kernels for 0%

commit v1 on v0

v1 whole, which is shorter than its diff:
```python
import jax
import jax.numpy as jnp
from jax import lax
from jax.experimental import pallas as pl
from jax.experimental.pallas import tpu as pltpu
from jax.sharding import PartitionSpec as P

FACTOR = 4
time_step = 0.25
diffusion_substrate = 0.16
diffusion_catalyst = 0.08

MESH = pl.DeviceIdType.MESH
F32 = jnp.float32

STATE, COEF, ENDS, START, DEFECT, MIDDLE, TRAIL = 0, 4, 5, 9, 10, 17, 18
FIELDS = 24
SLOTS = 4
LAST_PACK = 18


def place(x, r, group):
    snake = r < 12
    y = jnp.where(snake, lax.div(r, 3), 15 - r)
    t = lax.rem(r, 3)
    q = jnp.where(snake, jnp.where(lax.rem(y, 2) == 0, 1 + t, 3 - t), 0)
    z = 4 * lax.div(group, 2) + q
    core = 1 - lax.rem(group, 2)
    return y * 4 + lax.rem(z, 2) * 2 + core, x * 4 + lax.div(z, 2)


def roll(value, by, axis):
    return pltpu.roll(value, by % value.shape[axis], axis)


def kernel(
    initial, estimate, feed, kill, corrected, residual,
    field, land, pack, coef, work, late, coarse, back, diff, zero,
    halo_in, halo_out, block_in, block_out, first_out, coef_out, diff_out, corr_out,
    diff_in, corr_in, back_in, back_out, zero_sem,
):
    tm = lax.axis_index("tm")
    space = lax.axis_index("space")
    x, z_hi = lax.div(space, 4), lax.rem(space, 4)
    y, z_lo, core = lax.div(tm, 4), lax.rem(lax.div(tm, 2), 2), lax.rem(tm, 2)
    z = 2 * z_hi + z_lo
    cube, q = lax.div(z, 4), lax.rem(z, 4)
    r = jnp.where(q == 0, 15 - y, 3 * y + jnp.where(lax.rem(y, 2) == 0, q - 1, 3 - q))
    group = 2 * cube + 1 - core
    x_up, x_down = lax.rem(x + 1, 4), lax.rem(x + 3, 4)
    r_up, r_down = lax.rem(r + 1, 16), lax.rem(r + 15, 16)

    barrier = pltpu.get_barrier_semaphore()

    def greet(target):
        pl.semaphore_signal(barrier, inc=1, device_id=target, device_id_type=MESH)

    me = tm * 4 + z_hi

    @pl.loop(1, 64)
    def _(i):
        other = lax.rem(me + i, 64)
        greet((lax.div(other, 4), x * 4 + lax.rem(other, 4)))

    for side in (x_up, x_down):
        for row in (r_down, r, r_up):
            for other in range(4):
                greet(place(side, row, other))
    pl.semaphore_wait(barrier, 63 + 24)

    def is_me(target):
        return jnp.logical_and(target[0] == tm, target[1] == space)

    def put(src, dst, out_sem, in_sem, target):
        same = is_me(target)

        @pl.when(same)
        def _():
            pltpu.make_async_copy(src, dst, in_sem).start()

        @pl.when(jnp.logical_not(same))
        def _():
            pltpu.make_async_remote_copy(src, dst, out_sem, in_sem, device_id=target, device_id_type=MESH).start()

    def put_done(src, out_sem, target):
        @pl.when(jnp.logical_not(is_me(target)))
        def _():
            pltpu.make_async_copy(src, src, out_sem).wait()

    def rows_of(row):
        return pl.ds(pl.multiple_of(row * 8, 8), 8)

    here = pl.ds(4 + 2 * z_hi, 2)
    turn = lax.rem(tm + 1, 16)
    slot_there, group_there = lax.rem(turn, 4), lax.div(turn, 4)
    coef_row = jnp.where(lax.rem(tm, 4) == 0, 15 - y, 3 * y + jnp.where(lax.rem(y, 2) == 0, lax.rem(tm, 4) - 1, 3 - lax.rem(tm, 4)))

    def coef_put(other):
        target = place(x, coef_row, other)
        for k, src in enumerate((feed, kill)):
            put(src.at[:, rows_of(coef_row), :], field.at[COEF, k, here, 0:8, :], coef_out.at[other, k], block_in.at[COEF], target)

    for other in range(4):
        coef_put(other)

    def first_put(src):
        @pl.loop(0, 16)
        def _(i):
            row = lax.rem(r + i, 16)
            put(
                src.at[:, :, rows_of(row), :], field.at[slot_there, :, here, 0:8, :],
                first_out.at[i], block_in.at[slot_there], place(x, row, group_there),
            )

    @pl.when(tm < 15)
    def _():
        first_put(estimate.at[0])

    @pl.when(tm == 15)
    def _():
        first_put(initial)

    @pl.when(tm == 0)
    def _():
        zero[...] = jnp.zeros_like(zero)
        pltpu.make_async_copy(zero, residual.at[0], zero_sem).start()

    low = lax.broadcasted_iota(jnp.int32, (8, 128), 0)
    half = low < 4

    def block_of(f):
        return field.at[f, :, 4:12, 0:8, :]

    def send_halo(f, p, there, target_group):
        for k in range(2):
            plane = [field[f, k, 4 + b, 0:8, :] for b in range(8)]
            for t in range(4):
                a, b = plane[2 * t], plane[2 * t + 1]
                pack[p, 0, k, t] = jnp.where(half, a, roll(b, 4, 0))
                pack[p, 1, k, t] = jnp.where(half, roll(a, 4, 0), b)
            for side, near in ((0, (7, 6, 5)), (1, (0, 1, 2))):
                a, b, c = (plane[n] for n in near)
                pack[p, 2, k, 2 * side] = jnp.where(low < 3, a, jnp.where(low < 5, roll(b, 3, 0), roll(c, 5, 0)))
                pack[p, 2, k, 2 * side + 1] = jnp.where(low >= 5, a, jnp.where(low >= 3, roll(b, 5, 0), roll(c, 3, 0)))

        def send(src, dst, row, side):
            pltpu.make_async_remote_copy(
                src, dst, halo_out.at[p], halo_in.at[there],
                device_id=place(side, row, target_group), device_id_type=MESH,
            ).start()

        send(pack.at[p, 2, :, 0], land.at[there, 4, :, 0], r_down, x_up)
        send(pack.at[p, 2, :, 1], land.at[there, 4, :, 1], r_up, x_up)
        send(pack.at[p, 2, :, 2], land.at[there, 4, :, 2], r_down, x_down)
        send(pack.at[p, 2, :, 3], land.at[there, 4, :, 3], r_up, x_down)
        send(field.at[f, :, 8:12, 0:8, :], land.at[there, 0], r, x_up)
        send(field.at[f, :, 4:8, 0:8, :], land.at[there, 1], r, x_down)
        send(pack.at[p, 0], land.at[there, 2], r_down, x)
        send(pack.at[p, 1], land.at[there, 3], r_up, x)

    def wait_on(ref, sem):
        pltpu.make_async_copy(ref, ref, sem).wait()

    def receive_halo(f):
        wait_on(land.at[f], halo_in.at[f])
        for k in range(2):
            for n in range(4):
                field[f, k, n, 0:8, :] = land[f, 0, k, n]
                field[f, k, 12 + n, 0:8, :] = land[f, 1, k, n]
            for t in range(4):
                a, b = land[f, 2, k, t], land[f, 3, k, t]
                field[f, k, 4 + 2 * t, 8:16, :] = jnp.where(half, a, roll(b, 4, 0))
                field[f, k, 5 + 2 * t, 8:16, :] = jnp.where(half, roll(a, 4, 0), b)
            for side, near in ((0, (3, 2, 1)), (1, (12, 13, 14))):
                a, b = land[f, 4, k, 2 * side], land[f, 4, k, 2 * side + 1]
                field[f, k, near[0], 8:16, :] = jnp.where(half, a, b)
                field[f, k, near[1], 8:16, :] = jnp.where(half, roll(a, 5, 0), roll(b, 3, 0))
                field[f, k, near[2], 8:16, :] = jnp.where(half, roll(a, 3, 0), roll(b, 5, 0))

    def sums(get, p, rows):
        result = []
        for k in range(2):
            m = get(k, p)
            c = m[:rows]
            s = get(k, p - 1)[:rows] + get(k, p + 1)[:rows]
            s = s + (roll(m, 1, 0)[:rows] + roll(m, -1, 0)[:rows])
            s = s + (roll(c, 1, 1) + roll(c, -1, 1))
            result.append((c, s))
        return result

    def update(middles, which, p, rows, h):
        (u, su), (v, sv) = middles
        reaction = (h * u) * (v * v) if h != 1.0 else u * (v * v)
        fa, fb, fc = (coef[which, n, p][:rows] for n in range(3))
        new_u = (fa * u + (h * diffusion_substrate) * su) + (fb - reaction)
        new_v = (fc * v + (h * diffusion_catalyst) * sv) + reaction
        return new_u, new_v

    def fine_step(get, store, lo, hi, whole):
        for p in range(lo, hi):
            rows = 16 if whole and lo < p < hi - 1 else 8
            new_u, new_v = update(sums(get, p, rows), 0, p, rows, time_step)
            store(0, p, rows, new_u)
            store(1, p, rows, new_v)

    def from_field(f):
        return lambda k, p: field[f, k, p]

    def from_work(w):
        return lambda k, p: work[w, k, p]

    def to_work(w):
        def store(k, p, rows, value):
            work[w, k, p, 0:rows, :] = value

        return store

    wait_on(block_of(COEF), block_in.at[COEF])
    send_halo(COEF, COEF, COEF, group)

    @pl.loop(0, SLOTS)
    def _(s):
        wait_on(block_of(s), block_in.at[s])
        send_halo(s, s, s, group)

    receive_halo(COEF)
    for which, h in ((0, time_step), (1, time_step * FACTOR)):
        for p in range(16):
            f, g = field[COEF, 0, p], field[COEF, 1, p]
            coef[which, 0, p] = (1.0 - 6.0 * h * diffusion_substrate) - h * f
            coef[which, 1, p] = h * f
            coef[which, 2, p] = (1.0 - 6.0 * h * diffusion_catalyst) - h * (f + g)

    @pl.loop(0, SLOTS)
    def _(s):
        receive_halo(s)
        fine_step(from_field(s), to_work(0), 1, 15, True)
        fine_step(from_work(0), to_work(1), 2, 14, True)
        fine_step(from_work(1), to_work(0), 3, 13, True)

        def store(k, p, rows, value):
            field[ENDS + s, k, p, 0:8, :] = value

        fine_step(from_work(0), store, 4, 12, False)
        send_halo(ENDS + s, ENDS + s, ENDS + s, group)

    my_rows = rows_of(r)

    def owner(turn_index, part):
        return turn_index, x * 4 + part

    def corrected_put(f, n, turn_index):
        for part in range(4):
            put(
                field.at[f, :, 4 + 2 * part : 6 + 2 * part, 0:8, :], corrected.at[0, :, :, my_rows, :],
                corr_out.at[n, part], corr_in, owner(turn_index, part),
            )

    def corrected_done(f, n, turn_index):
        for part in range(4):
            put_done(field.at[f, :, 4 + 2 * part : 6 + 2 * part, 0:8, :], corr_out.at[n, part], owner(turn_index, part))

    def residual_put(s):
        for part in range(4):
            put(
                diff.at[s, :, 2 * part : 2 * part + 2], residual.at[0, :, :, my_rows, :],
                diff_out.at[s, part], diff_in, owner(4 * group + s, part),
            )

    def residual_done(s):
        for part in range(4):
            put_done(diff.at[s, :, 2 * part : 2 * part + 2], diff_out.at[s, part], owner(4 * group + s, part))

    chain = core == 1
    chain_group = 2 * cube

    def defect_field(s):
        return jnp.where(cube == 0, START, DEFECT - 8) + 4 * group + s

    def has_halo(f):
        return jnp.logical_and(f != DEFECT + 3, f < DEFECT + 6)

    @pl.loop(0, SLOTS)
    def _(s):
        f = defect_field(s)
        receive_halo(ENDS + s)
        for p in range(1, 15):
            rows = 16 if 1 < p < 14 else 8
            middles = sums(from_field(ENDS + s), p, rows)
            new_u, new_v = update(middles, 0, p, rows, time_step)
            work[0, 0, p, 0:rows, :] = new_u
            work[0, 1, p, 0:rows, :] = new_v
            if 4 <= p < 12:
                new_u, new_v = update([(c[:8], w[:8]) for c, w in middles], 1, p, 8, time_step * FACTOR)
                coarse[0, p - 4] = new_u
                coarse[1, p - 4] = new_v
        fine_step(from_work(0), to_work(1), 2, 14, True)
        fine_step(from_work(1), to_work(0), 3, 13, True)
        opening = jnp.logical_and(group == 0, s == 0)
        following = jnp.minimum(s + 1, SLOTS - 1)

        def store(k, p, rows, value):
            late[s, k, p - 4] = value
            field[f, k, p, 0:8, :] = value - jnp.where(opening, 0.0, coarse[k, p - 4])
            diff[s + 1, k, p - 4] = value - field[ENDS + following, k, p, 0:8, :]

        fine_step(from_work(0), store, 4, 12, False)

        @pl.when(has_halo(f))
        def _():
            send_halo(f, f, f, chain_group)

        @pl.when(jnp.logical_and(core == 0, f < DEFECT + 7))
        def _():
            pltpu.make_async_remote_copy(
                block_of(f), block_of(f), block_out.at[f], block_in.at[f],
                device_id=place(x, r, chain_group), device_id_type=MESH,
            ).start()

        @pl.when(s < SLOTS - 1)
        def _():
            residual_put(s + 1)

        @pl.when(jnp.logical_and(s == SLOTS - 1, group < 3))
        def _():
            pltpu.make_async_remote_copy(
                late.at[s], back, back_out, back_in, device_id=place(x, r, group + 1), device_id_type=MESH
            ).start()

    def coarse_step(src, dst, d, lo, hi, whole):
        for p in range(lo, hi):
            rows = 16 if whole and lo < p < hi - 1 else 8
            new_u, new_v = update(sums(from_field(src), p, rows), 1, p, rows, time_step * FACTOR)
            field[dst, 0, p, 0:rows, :] = new_u + field[d, 0, p, 0:rows, :]
            field[dst, 1, p, 0:rows, :] = new_v + field[d, 1, p, 0:rows, :]

    steps = (START, TRAIL, TRAIL + 1, TRAIL + 2, MIDDLE, TRAIL + 3, TRAIL + 4, TRAIL + 5)
    first_turn = jnp.where(cube == 0, 1, 8)

    def first_residual():
        wait_on(back, back_in)
        for k in range(2):
            for b in range(8):
                diff[0, k, b] = back[k, b] - field[ENDS, k, 4 + b, 0:8, :]
        residual_put(0)

    @pl.when(chain)
    def _():
        @pl.when(cube == 0)
        def _():
            corrected_put(ENDS, 8, 0)

        @pl.when(cube == 1)
        def _():
            first_residual()

        for n in range(3):
            receive_halo(DEFECT + n)
        receive_halo(START)

        @pl.when(cube == 1)
        def _():
            wait_on(block_of(START), block_in.at[START])

        coarse_step(steps[0], steps[1], DEFECT, 1, 15, True)
        coarse_step(steps[1], steps[2], DEFECT + 1, 2, 14, True)
        coarse_step(steps[2], steps[3], DEFECT + 2, 3, 13, True)

        @pl.when(cube == 0)
        def _():
            wait_on(block_of(DEFECT + 3), block_in.at[DEFECT + 3])

        coarse_step(steps[3], steps[4], DEFECT + 3, 4, 12, False)
        send_halo(MIDDLE, MIDDLE, MIDDLE, group)

        @pl.when(cube == 0)
        def _():
            corrected_put(START, 0, 1)

        for n in range(1, 5):
            corrected_put(steps[n], n, first_turn + n)
        for n in range(4, 7):
            wait_on(block_of(DEFECT + n), block_in.at[DEFECT + n])
        for n in range(4, 6):
            receive_halo(DEFECT + n)
        receive_halo(MIDDLE)
        coarse_step(steps[4], steps[5], DEFECT + 4, 2, 14, True)
        coarse_step(steps[5], steps[6], DEFECT + 5, 3, 13, True)
        coarse_step(steps[6], steps[7], DEFECT + 6, 4, 12, False)

        @pl.when(cube == 0)
        def _():
            send_halo(steps[7], LAST_PACK, START, 2)
            pltpu.make_async_remote_copy(
                block_of(steps[7]), block_of(START), block_out.at[START], block_in.at[START],
                device_id=place(x, r, 2), device_id_type=MESH,
            ).start()

        for n in range(5, 8):
            corrected_put(steps[n], n, first_turn + n)

    @pl.when(core == 0)
    def _():
        first_residual()

    for other in range(4):
        for k, src in enumerate((feed, kill)):
            put_done(src.at[:, rows_of(coef_row), :], coef_out.at[other, k], place(x, coef_row, other))

    @pl.loop(0, 16)
    def _(i):
        row = lax.rem(r + i, 16)
        put_done(initial.at[:, :, rows_of(row), :], first_out.at[i], place(x, row, group_there))

    @pl.loop(0, ENDS + SLOTS)
    def _(f):
        wait_on(land.at[f], halo_out.at[f])

    @pl.loop(0, SLOTS)
    def _(s):
        f = defect_field(s)

        @pl.when(has_halo(f))
        def _():
            wait_on(land.at[f], halo_out.at[f])

        @pl.when(jnp.logical_and(core == 0, f < DEFECT + 7))
        def _():
            wait_on(block_of(f), block_out.at[f])

        @pl.when(4 * group + s > 0)
        def _():
            residual_done(s)

    @pl.when(group < 3)
    def _():
        wait_on(back, back_out)

    @pl.when(chain)
    def _():
        wait_on(land.at[MIDDLE], halo_out.at[MIDDLE])

        @pl.when(cube == 0)
        def _():
            wait_on(land.at[START], halo_out.at[LAST_PACK])
            wait_on(block_of(START), block_out.at[START])
            corrected_done(ENDS, 8, 0)
            corrected_done(START, 0, 1)

        for n in range(1, 8):
            corrected_done(steps[n], n, first_turn + n)

    wait_on(corrected, corr_in)

    @pl.when(tm > 0)
    def _():
        wait_on(residual, diff_in)

    @pl.when(tm == 0)
    def _():
        wait_on(residual.at[0], zero_sem)


def on_device(initial, estimate, feed_rate, kill_rate):
    dma = pltpu.SemaphoreType.DMA
    vmem = pltpu.VMEM
    return pl.pallas_call(
        kernel,
        out_shape=(jax.ShapeDtypeStruct(estimate.shape, F32), jax.ShapeDtypeStruct(estimate.shape, F32)),
        in_specs=[pl.BlockSpec(memory_space=pl.ANY)] * 4,
        out_specs=[pl.BlockSpec(memory_space=pl.ANY)] * 2,
        scratch_shapes=[
            vmem((FIELDS, 2, 16, 16, 128), F32),
            vmem((TRAIL, 5, 2, 4, 8, 128), F32),
            vmem((LAST_PACK + 1, 3, 2, 4, 8, 128), F32),
            vmem((2, 3, 16, 16, 128), F32),
            vmem((2, 2, 16, 16, 128), F32),
            vmem((SLOTS, 2, 8, 8, 128), F32),
            vmem((2, 8, 8, 128), F32),
            vmem((2, 8, 8, 128), F32),
            vmem((SLOTS + 1, 2, 8, 8, 128), F32),
            vmem((2, 2, 128, 128), F32),
            dma((TRAIL,)), dma((LAST_PACK + 1,)), dma((TRAIL,)), dma((TRAIL,)),
            dma((16,)), dma((4, 2)), dma((SLOTS, 4)), dma((9, 4)),
            dma, dma, dma, dma, dma,
        ],
        compiler_params=pltpu.CompilerParams(
            collective_id=0, has_side_effects=True, vmem_limit_bytes=40 * 1024 * 1024
        ),
        name="mgrit_cycle",
    )(initial, estimate, feed_rate, kill_rate)


def solution(mesh):
    placed = (
        P(None, "space", None, None),
        P("tm", None, "space", None, None),
        P("space", None, None),
        P("space", None, None),
    )
    return jax.shard_map(
        on_device,
        mesh=mesh,
        in_specs=placed,
        out_specs=(P("tm", None, "space", None, None), P("tm", None, "space", None, None)),
        check_vma=False,
    )
```

time: 457 us -> 73 us (0.16)
  the two profiles are of different devices: /device:TPU:22 before, /device:TPU:57 now
where the time goes in v1:
time: 73 us; the launch traced here: 72.9 us
  Pallas kernels  67.1 us (92%)
  local copies, waits for them, and re-layouts  5.11 us (7%)
    pallas_call x1, Pallas kernels, on_device(): pl.pallas_call(kernel, out_shape=(jax.ShapeDtypeStruct(estimate.shape, F3...  67.1 us
    unnamed x10, local copies, waits for them, and re-layouts  5.11 us

profile of v1, /device:TPU:57, one launch (start us, length us, event | category | flops | bytes accessed | tf_op | source)
XLA Modules:
  0.0 72.9 jit_solution(5290538057784560645)
XLA Ops:
  0.6 0.0 copy-start
  0.6 0.9 %copy-done = f32[2,2,128,128]{3,2,1,0:T(8,128)S(1)} copy-done((f32[2,2,128,128]{3,2,1,0:T(8,128)S(1)}, f32[2,2,128,128]{3,2,1,0:T(8,128)}, u32[]{:S(2)}) %copy-start) | copy-done | bytes 262168
  1.6 0.0 copy-start.1
  1.6 0.9 %copy-done.1 = f32[1,2,2,128,128]{4,3,2,1,0:T(8,128)S(1)} copy-done((f32[1,2,2,128,128]{4,3,2,1,0:T(8,128)S(1)}, f32[1,2,2,128,128]{4,3,2,1,0:T(8,128)}, u32[]{:S(2)}) %copy-start.1) | copy-done | bytes 262168
  2.5 0.0 copy-start.2
  2.5 0.9 %copy-done.2 = f32[2,128,128]{2,1,0:T(8,128)S(1)} copy-done((f32[2,128,128]{2,1,0:T(8,128)S(1)}, f32[2,128,128]{2,1,0:T(8,128)}, u32[]{:S(2)}) %copy-start.2) | copy-done | bytes 131096
  3.4 0.0 copy-start.3
  3.4 0.9 %copy-done.3 = f32[2,128,128]{2,1,0:T(8,128)S(1)} copy-done((f32[2,128,128]{2,1,0:T(8,128)S(1)}, f32[2,128,128]{2,1,0:T(8,128)}, u32[]{:S(2)}) %copy-start.3) | copy-done | bytes 131096
  4.3 67.1 %mgrit_cycle.1 = (f32[1,2,2,128,128]{4,3,2,1,0:T(8,128)S(1)}, f32[1,2,2,128,128]{4,3,2,1,0:T(8,128)S(1)}) custom-call(f32[2,2,128,128]{3,2,1,0:T(8,128)S(1)} %copy-done, f32[1,2,2,128,128]{4,3,2,1,0:T(8,128)S(1)} %copy-done.1, f32[2,128,128]{2,1,0:T(8,128)S(1)} %copy-done.2, f32[2,128,128]{2,1,0:T(8,128)S(1)} %copy-done.3), custom_call_target="tpu_custom_call" | custom-call | tf_op jit(solution)/shard_map/mgrit_cycle/pallas_call | solution.py:467
  71.5 0.7 copy.8
  72.2 0.7 copy.9
Async XLA Ops:
  0.6 1.0 %copy-start = (f32[2,2,128,128]{3,2,1,0:T(8,128)S(1)}, f32[2,2,128,128]{3,2,1,0:T(8,128)}, u32[]{:S(2)}) copy-start(f32[2,2,128,128]{3,2,1,0:T(8,128)} %initial.1) | copy-start | bytes 786436
  1.6 0.9 %copy-start.1 = (f32[1,2,2,128,128]{4,3,2,1,0:T(8,128)S(1)}, f32[1,2,2,128,128]{4,3,2,1,0:T(8,128)}, u32[]{:S(2)}) copy-start(f32[1,2,2,128,128]{4,3,2,1,0:T(8,128)} %estimate.1) | copy-start | bytes 786436
  2.5 0.9 %copy-start.2 = (f32[2,128,128]{2,1,0:T(8,128)S(1)}, f32[2,128,128]{2,1,0:T(8,128)}, u32[]{:S(2)}) copy-start(f32[2,128,128]{2,1,0:T(8,128)} %feed.1) | copy-start | bytes 393220
  3.4 0.9 %copy-start.3 = (f32[2,128,128]{2,1,0:T(8,128)S(1)}, f32[2,128,128]{2,1,0:T(8,128)}, u32[]{:S(2)}) copy-start(f32[2,128,128]{2,1,0:T(8,128)} %kill.1) | copy-start | bytes 393220

commit v2 on v1

--- a/solution.py
+++ b/solution.py
@@ -20,13 +20,9 @@
 
 
 def place(x, r, group):
-    snake = r < 12
-    y = jnp.where(snake, lax.div(r, 3), 15 - r)
-    t = lax.rem(r, 3)
-    q = jnp.where(snake, jnp.where(lax.rem(y, 2) == 0, 1 + t, 3 - t), 0)
-    z = 4 * lax.div(group, 2) + q
-    core = 1 - lax.rem(group, 2)
-    return y * 4 + lax.rem(z, 2) * 2 + core, x * 4 + lax.div(z, 2)
+    y = 2 * lax.div(group, 2) + lax.div(r, 8)
+    z = jnp.where(r < 8, r, 15 - r)
+    return y * 4 + lax.rem(z, 2) * 2 + 1 - lax.rem(group, 2), x * 4 + lax.div(z, 2)
 
 
 def roll(value, by, axis):
@@ -44,9 +40,9 @@
     x, z_hi = lax.div(space, 4), lax.rem(space, 4)
     y, z_lo, core = lax.div(tm, 4), lax.rem(lax.div(tm, 2), 2), lax.rem(tm, 2)
     z = 2 * z_hi + z_lo
-    cube, q = lax.div(z, 4), lax.rem(z, 4)
-    r = jnp.where(q == 0, 15 - y, 3 * y + jnp.where(lax.rem(y, 2) == 0, q - 1, 3 - q))
-    group = 2 * cube + 1 - core
+    late_half = lax.div(y, 2)
+    r = jnp.where(lax.rem(y, 2) == 0, z, 15 - z)
+    group = 2 * late_half + 1 - core
     x_up, x_down = lax.rem(x + 1, 4), lax.rem(x + 3, 4)
     r_up, r_down = lax.rem(r + 1, 16), lax.rem(r + 15, 16)
 
@@ -93,15 +89,16 @@
     here = pl.ds(4 + 2 * z_hi, 2)
     turn = lax.rem(tm + 1, 16)
     slot_there, group_there = lax.rem(turn, 4), lax.div(turn, 4)
-    coef_row = jnp.where(lax.rem(tm, 4) == 0, 15 - y, 3 * y + jnp.where(lax.rem(y, 2) == 0, lax.rem(tm, 4) - 1, 3 - lax.rem(tm, 4)))
-
-    def coef_put(other):
-        target = place(x, coef_row, other)
+
+    def coef_place(n):
+        there = lax.rem(jnp.where(z_lo == 1, z + n, z + 8 - n), 8)
+        row = jnp.where(lax.rem(y, 2) == 0, there, 15 - there)
+        return row, (y * 4 + lax.rem(there, 2) * 2 + core, x * 4 + lax.div(there, 2))
+
+    for n in range(4):
+        row, target = coef_place(n)
         for k, src in enumerate((feed, kill)):
-            put(src.at[:, rows_of(coef_row), :], field.at[COEF, k, here, 0:8, :], coef_out.at[other, k], block_in.at[COEF], target)
-
-    for other in range(4):
-        coef_put(other)
+            put(src.at[:, rows_of(row), :], field.at[COEF, k, here, 0:8, :], coef_out.at[n, k], block_in.at[COEF], target)
 
     def first_put(src):
         @pl.loop(0, 16)
@@ -272,10 +269,10 @@
             put_done(diff.at[s, :, 2 * part : 2 * part + 2], diff_out.at[s, part], owner(4 * group + s, part))
 
     chain = core == 1
-    chain_group = 2 * cube
+    chain_group = 2 * late_half
 
     def defect_field(s):
-        return jnp.where(cube == 0, START, DEFECT - 8) + 4 * group + s
+        return jnp.where(late_half == 0, START, DEFECT - 8) + 4 * group + s
 
     def has_halo(f):
         return jnp.logical_and(f != DEFECT + 3, f < DEFECT + 6)
@@ -335,7 +332,7 @@
             field[dst, 1, p, 0:rows, :] = new_v + field[d, 1, p, 0:rows, :]
 
     steps = (START, TRAIL, TRAIL + 1, TRAIL + 2, MIDDLE, TRAIL + 3, TRAIL + 4, TRAIL + 5)
-    first_turn = jnp.where(cube == 0, 1, 8)
+    first_turn = jnp.where(late_half == 0, 1, 8)
 
     def first_residual():
         wait_on(back, back_in)
@@ -346,11 +343,11 @@
 
     @pl.when(chain)
     def _():
-        @pl.when(cube == 0)
+        @pl.when(late_half == 0)
         def _():
             corrected_put(ENDS, 8, 0)
 
-        @pl.when(cube == 1)
+        @pl.when(late_half == 1)
         def _():
             first_residual()
 
@@ -358,7 +355,7 @@
             receive_halo(DEFECT + n)
         receive_halo(START)
 
-        @pl.when(cube == 1)
+        @pl.when(late_half == 1)
         def _():
             wait_on(block_of(START), block_in.at[START])
 
@@ -366,14 +363,14 @@
         coarse_step(steps[1], steps[2], DEFECT + 1, 2, 14, True)
         coarse_step(steps[2], steps[3], DEFECT + 2, 3, 13, True)
 
-        @pl.when(cube == 0)
+        @pl.when(late_half == 0)
         def _():
             wait_on(block_of(DEFECT + 3), block_in.at[DEFECT + 3])
 
         coarse_step(steps[3], steps[4], DEFECT + 3, 4, 12, False)
         send_halo(MIDDLE, MIDDLE, MIDDLE, group)
 
-        @pl.when(cube == 0)
+        @pl.when(late_half == 0)
         def _():
             corrected_put(START, 0, 1)
 
@@ -388,7 +385,7 @@
         coarse_step(steps[5], steps[6], DEFECT + 5, 3, 13, True)
         coarse_step(steps[6], steps[7], DEFECT + 6, 4, 12, False)
 
-        @pl.when(cube == 0)
+        @pl.when(late_half == 0)
         def _():
             send_halo(steps[7], LAST_PACK, START, 2)
             pltpu.make_async_remote_copy(
@@ -403,9 +400,10 @@
     def _():
         first_residual()
 
-    for other in range(4):
+    for n in range(4):
+        row, target = coef_place(n)
         for k, src in enumerate((feed, kill)):
-            put_done(src.at[:, rows_of(coef_row), :], coef_out.at[other, k], place(x, coef_row, other))
+            put_done(src.at[:, rows_of(row), :], coef_out.at[n, k], target)
 
     @pl.loop(0, 16)
     def _(i):
@@ -440,7 +438,7 @@
     def _():
         wait_on(land.at[MIDDLE], halo_out.at[MIDDLE])
 
-        @pl.when(cube == 0)
+        @pl.when(late_half == 0)
         def _():
             wait_on(land.at[START], halo_out.at[LAST_PACK])
             wait_on(block_of(START), block_out.at[START])
@@ -485,7 +483,7 @@
             dma, dma, dma, dma, dma,
         ],
         compiler_params=pltpu.CompilerParams(
-            collective_id=0, has_side_effects=True, vmem_limit_bytes=40 * 1024 * 1024
+            collective_id=0, has_side_effects=True, vmem_limit_bytes=63 * 1024 * 1024
         ),
         name="mgrit_cycle",
     )(initial, estimate, feed_rate, kill_rate)

time: 73 us -> 63.9 us (0.88)
  Pallas kernels: 67.1 us -> 60.7 us
  local copies, waits for them, and re-layouts: 5.11 us -> 2.42 us
    pallas_call x1, Pallas kernels: 67.1 us -> 60.7 us  [on_device(): pl.pallas_call(kernel, out_shape=(jax.ShapeDtypeStruct(estimate.shape, F3...]
    unnamed x10 -> x4, local copies, waits for them, and re-layouts: 5.11 us -> 2.42 us
where the time goes in v2:
time: 63.9 us; the launch traced here: 63.8 us
  Pallas kernels  60.7 us (95%)
  local copies, waits for them, and re-layouts  2.42 us (4%)
  between operations  0.65 us (1%)
    pallas_call x1, Pallas kernels, on_device(): pl.pallas_call(kernel, out_shape=(jax.ShapeDtypeStruct(estimate.shape, F3...  60.7 us
    unnamed x4, local copies, waits for them, and re-layouts  2.42 us

profile of v2, /device:TPU:57, one launch (start us, length us, event | category | flops | bytes accessed | tf_op | source)
XLA Modules:
  0.0 63.8 jit_solution(16237119390510451357)
XLA Ops:
  0.6 60.7 %mgrit_cycle.1 = (f32[1,2,2,128,128]{4,3,2,1,0:T(8,128)}, f32[1,2,2,128,128]{4,3,2,1,0:T(8,128)}) custom-call(f32[2,2,128,128]{3,2,1,0:T(8,128)} %initial.1, f32[1,2,2,128,128]{4,3,2,1,0:T(8,128)} %estimate.1, f32[2,128,128]{2,1,0:T(8,128)} %feed.1, f32[2,128,128]{2,1,0:T(8,128)} %kill.1), custom_call_target="tpu_custom_call" | custom-call | tf_op jit(solution)/shard_map/mgrit_cycle/pallas_call | solution.py:465
  61.3 0.0 copy-start
  61.4 1.7 %copy.8 = f32[1,2,2,128,128]{4,3,2,1,0:T(8,128)} copy(f32[1,2,2,128,128]{4,3,2,1,0:T(8,128)} %get-tuple-element.4) | data formatting | bytes 524288
  63.1 0.0 copy-done
  63.1 0.7 %copy.9 = f32[1,2,2,128,128]{4,3,2,1,0:T(8,128)} copy(f32[1,2,2,128,128]{4,3,2,1,0:T(8,128)S(1)} %copy-done) | data formatting | bytes 524288
Async XLA Ops:
  61.3 1.7 %copy-start = (f32[1,2,2,128,128]{4,3,2,1,0:T(8,128)S(1)}, f32[1,2,2,128,128]{4,3,2,1,0:T(8,128)}, u32[]{:S(2)}) copy-start(f32[1,2,2,128,128]{4,3,2,1,0:T(8,128)} %get-tuple-element.5) | copy-start | bytes 786436

commit v3 on v2

--- a/solution.py
+++ b/solution.py
@@ -30,11 +30,12 @@
 
 
 def kernel(
-    initial, estimate, feed, kill, corrected, residual,
+    initial, estimate, feed, kill, both,
     field, land, pack, coef, work, late, coarse, back, diff, zero,
     halo_in, halo_out, block_in, block_out, first_out, coef_out, diff_out, corr_out,
-    diff_in, corr_in, back_in, back_out, zero_sem,
+    diff_in, corr_in, back_in, back_out, zero_sem, go,
 ):
+    corrected, residual = both.at[0], both.at[1]
     tm = lax.axis_index("tm")
     space = lax.axis_index("space")
     x, z_hi = lax.div(space, 4), lax.rem(space, 4)
@@ -46,26 +47,60 @@
     x_up, x_down = lax.rem(x + 1, 4), lax.rem(x + 3, 4)
     r_up, r_down = lax.rem(r + 1, 16), lax.rem(r + 15, 16)
 
+    near = {}
+    for dx, side in ((-1, x_down), (0, x), (1, x_up)):
+        for dr, row in ((-1, r_down), (0, r), (1, r_up)):
+            near[dx, dr] = place(side, row, 2 * late_half + 1)
+
+    def neighbour(dx, dr, offset):
+        base, part = near[dx, dr]
+        return base + offset, part
+
     barrier = pltpu.get_barrier_semaphore()
+
+    def is_me(target):
+        return jnp.logical_and(target[0] == tm, target[1] == space)
+
+    turn = lax.rem(tm + 1, 16)
+    slot_there, group_there = lax.rem(turn, 4), lax.div(turn, 4)
 
     def greet(target):
         pl.semaphore_signal(barrier, inc=1, device_id=target, device_id_type=MESH)
 
-    me = tm * 4 + z_hi
-
-    @pl.loop(1, 64)
+    def greet_other(target):
+        @pl.when(jnp.logical_not(is_me(target)))
+        def _():
+            greet(target)
+
+    @pl.loop(0, 16)
     def _(i):
-        other = lax.rem(me + i, 64)
-        greet((lax.div(other, 4), x * 4 + lax.rem(other, 4)))
-
-    for side in (x_up, x_down):
-        for row in (r_down, r, r_up):
-            for other in range(4):
-                greet(place(side, row, other))
-    pl.semaphore_wait(barrier, 63 + 24)
-
-    def is_me(target):
-        return jnp.logical_and(target[0] == tm, target[1] == space)
+        greet_other((lax.rem(4 * group + lax.div(i, 4) + 15, 16), x * 4 + lax.rem(i, 4)))
+
+    ahead = 2 * z_lo - 1
+    for n in (1, -2, 3):
+        there = lax.rem(z + n * ahead + 8, 8)
+        greet((y * 4 + lax.rem(there, 2) * 2 + core, x * 4 + lax.div(there, 2)))
+
+    for dx in (-1, 0, 1):
+        for dr in (-1, 0, 1):
+            if dx or dr:
+                greet(neighbour(dx, dr, core))
+    greet((tm + 1 - 2 * core, space))
+
+    @pl.when(jnp.logical_and(late_half == 1, core == 1))
+    def _():
+        greet((tm - 8, space))
+        greet((tm - 9, space))
+
+    @pl.when(lax.rem(tm, 4) == 3)
+    def _():
+        @pl.loop(0, 16)
+        def _(i):
+            greet_other(place(x, i, lax.div(tm, 4)))
+
+    mine_there = (group_there == group).astype(jnp.int32)
+    mine_last = jnp.logical_and(lax.rem(tm, 4) == 3, lax.div(tm, 4) == group).astype(jnp.int32)
+    pl.semaphore_wait(barrier, (16 - mine_there) + 3 + 8 + 1 + (1 - late_half) + (4 - mine_last))
 
     def put(src, dst, out_sem, in_sem, target):
         same = is_me(target)
@@ -87,8 +122,6 @@
         return pl.ds(pl.multiple_of(row * 8, 8), 8)
 
     here = pl.ds(4 + 2 * z_hi, 2)
-    turn = lax.rem(tm + 1, 16)
-    slot_there, group_there = lax.rem(turn, 4), lax.div(turn, 4)
 
     def coef_place(n):
         there = lax.rem(jnp.where(z_lo == 1, z + n, z + 8 - n), 8)
@@ -100,10 +133,16 @@
         for k, src in enumerate((feed, kill)):
             put(src.at[:, rows_of(row), :], field.at[COEF, k, here, 0:8, :], coef_out.at[n, k], block_in.at[COEF], target)
 
+    def first_row(i):
+        n = lax.div(i, 2)
+        step = jnp.where(lax.rem(n, 2) == 1, 4 - lax.div(n + 1, 2), 4 + lax.div(n, 2))
+        there = lax.rem(z + step, 8)
+        return jnp.where(lax.rem(i, 2) == 0, there, 15 - there)
+
     def first_put(src):
         @pl.loop(0, 16)
         def _(i):
-            row = lax.rem(r + i, 16)
+            row = first_row(i)
             put(
                 src.at[:, :, rows_of(row), :], field.at[slot_there, :, here, 0:8, :],
                 first_out.at[i], block_in.at[slot_there], place(x, row, group_there),
@@ -128,7 +167,7 @@
     def block_of(f):
         return field.at[f, :, 4:12, 0:8, :]
 
-    def send_halo(f, p, there, target_group):
+    def send_halo(f, p, there, offset):
         for k in range(2):
             plane = [field[f, k, 4 + b, 0:8, :] for b in range(8)]
             for t in range(4):
@@ -140,20 +179,20 @@
                 pack[p, 2, k, 2 * side] = jnp.where(low < 3, a, jnp.where(low < 5, roll(b, 3, 0), roll(c, 5, 0)))
                 pack[p, 2, k, 2 * side + 1] = jnp.where(low >= 5, a, jnp.where(low >= 3, roll(b, 5, 0), roll(c, 3, 0)))
 
-        def send(src, dst, row, side):
+        def send(src, dst, dx, dr):
             pltpu.make_async_remote_copy(
                 src, dst, halo_out.at[p], halo_in.at[there],
-                device_id=place(side, row, target_group), device_id_type=MESH,
+                device_id=neighbour(dx, dr, offset), device_id_type=MESH,
             ).start()
 
-        send(pack.at[p, 2, :, 0], land.at[there, 4, :, 0], r_down, x_up)
-        send(pack.at[p, 2, :, 1], land.at[there, 4, :, 1], r_up, x_up)
-        send(pack.at[p, 2, :, 2], land.at[there, 4, :, 2], r_down, x_down)
-        send(pack.at[p, 2, :, 3], land.at[there, 4, :, 3], r_up, x_down)
-        send(field.at[f, :, 8:12, 0:8, :], land.at[there, 0], r, x_up)
-        send(field.at[f, :, 4:8, 0:8, :], land.at[there, 1], r, x_down)
-        send(pack.at[p, 0], land.at[there, 2], r_down, x)
-        send(pack.at[p, 1], land.at[there, 3], r_up, x)
+        send(pack.at[p, 2, :, 0], land.at[there, 4, :, 0], 1, -1)
+        send(pack.at[p, 2, :, 1], land.at[there, 4, :, 1], 1, 1)
+        send(pack.at[p, 2, :, 2], land.at[there, 4, :, 2], -1, -1)
+        send(pack.at[p, 2, :, 3], land.at[there, 4, :, 3], -1, 1)
+        send(field.at[f, :, 8:12, 0:8, :], land.at[there, 0], 1, 0)
+        send(field.at[f, :, 4:8, 0:8, :], land.at[there, 1], -1, 0)
+        send(pack.at[p, 0], land.at[there, 2], 0, -1)
+        send(pack.at[p, 1], land.at[there, 3], 0, 1)
 
     def wait_on(ref, sem):
         pltpu.make_async_copy(ref, ref, sem).wait()
@@ -213,12 +252,12 @@
         return store
 
     wait_on(block_of(COEF), block_in.at[COEF])
-    send_halo(COEF, COEF, COEF, group)
+    send_halo(COEF, COEF, COEF, core)
 
     @pl.loop(0, SLOTS)
     def _(s):
         wait_on(block_of(s), block_in.at[s])
-        send_halo(s, s, s, group)
+        send_halo(s, s, s, core)
 
     receive_halo(COEF)
     for which, h in ((0, time_step), (1, time_step * FACTOR)):
@@ -239,7 +278,7 @@
             field[ENDS + s, k, p, 0:8, :] = value
 
         fine_step(from_work(0), store, 4, 12, False)
-        send_halo(ENDS + s, ENDS + s, ENDS + s, group)
+        send_halo(ENDS + s, ENDS + s, ENDS + s, core)
 
     my_rows = rows_of(r)
 
@@ -276,6 +315,10 @@
 
     def has_halo(f):
         return jnp.logical_and(f != DEFECT + 3, f < DEFECT + 6)
+
+    @pl.when(group == 0)
+    def _():
+        corrected_put(ENDS, 8, 0)
 
     @pl.loop(0, SLOTS)
     def _(s):
@@ -305,7 +348,7 @@
 
         @pl.when(has_halo(f))
         def _():
-            send_halo(f, f, f, chain_group)
+            send_halo(f, f, f, 1)
 
         @pl.when(jnp.logical_and(core == 0, f < DEFECT + 7))
         def _():
@@ -314,7 +357,7 @@
                 device_id=place(x, r, chain_group), device_id_type=MESH,
             ).start()
 
-        @pl.when(s < SLOTS - 1)
+        @pl.when(jnp.logical_and(s < SLOTS - 1, late_half == 1))
         def _():
             residual_put(s + 1)
 
@@ -343,10 +386,6 @@
 
     @pl.when(chain)
     def _():
-        @pl.when(late_half == 0)
-        def _():
-            corrected_put(ENDS, 8, 0)
-
         @pl.when(late_half == 1)
         def _():
             first_residual()
@@ -368,33 +407,58 @@
             wait_on(block_of(DEFECT + 3), block_in.at[DEFECT + 3])
 
         coarse_step(steps[3], steps[4], DEFECT + 3, 4, 12, False)
-        send_halo(MIDDLE, MIDDLE, MIDDLE, group)
-
-        @pl.when(late_half == 0)
-        def _():
-            corrected_put(START, 0, 1)
-
-        for n in range(1, 5):
-            corrected_put(steps[n], n, first_turn + n)
+        send_halo(MIDDLE, MIDDLE, MIDDLE, core)
+
         for n in range(4, 7):
             wait_on(block_of(DEFECT + n), block_in.at[DEFECT + n])
+
+        @pl.when(late_half == 1)
+        def _():
+            for n in range(0, 5):
+                corrected_put(steps[n], n, first_turn + n)
+
         for n in range(4, 6):
             receive_halo(DEFECT + n)
         receive_halo(MIDDLE)
         coarse_step(steps[4], steps[5], DEFECT + 4, 2, 14, True)
+
+        @pl.when(late_half == 1)
+        def _():
+            corrected_put(steps[5], 5, first_turn + 5)
+
         coarse_step(steps[5], steps[6], DEFECT + 5, 3, 13, True)
+
+        @pl.when(late_half == 1)
+        def _():
+            corrected_put(steps[6], 6, first_turn + 6)
+
         coarse_step(steps[6], steps[7], DEFECT + 6, 4, 12, False)
 
         @pl.when(late_half == 0)
         def _():
-            send_halo(steps[7], LAST_PACK, START, 2)
+            send_halo(steps[7], LAST_PACK, START, 9)
             pltpu.make_async_remote_copy(
                 block_of(steps[7]), block_of(START), block_out.at[START], block_in.at[START],
                 device_id=place(x, r, 2), device_id_type=MESH,
             ).start()
-
-        for n in range(5, 8):
-            corrected_put(steps[n], n, first_turn + n)
+            pl.semaphore_signal(go, inc=1, device_id=(tm - 1, space), device_id_type=MESH)
+            for n in range(0, 7):
+                corrected_put(steps[n], n, first_turn + n)
+
+        @pl.when(late_half == 1)
+        def _():
+            corrected_put(steps[7], 7, first_turn + 7)
+
+        @pl.when(late_half == 0)
+        def _():
+            for n in range(1, SLOTS):
+                residual_put(n)
+
+    @pl.when(jnp.logical_and(core == 0, late_half == 0))
+    def _():
+        pl.semaphore_wait(go, 1)
+        for n in range(1, SLOTS):
+            residual_put(n)
 
     @pl.when(core == 0)
     def _():
@@ -407,7 +471,7 @@
 
     @pl.loop(0, 16)
     def _(i):
-        row = lax.rem(r + i, 16)
+        row = first_row(i)
         put_done(initial.at[:, :, rows_of(row), :], first_out.at[i], place(x, row, group_there))
 
     @pl.loop(0, ENDS + SLOTS)
@@ -443,9 +507,12 @@
             wait_on(land.at[START], halo_out.at[LAST_PACK])
             wait_on(block_of(START), block_out.at[START])
             corrected_done(ENDS, 8, 0)
-            corrected_done(START, 0, 1)
-
-        for n in range(1, 8):
+
+        @pl.when(late_half == 1)
+        def _():
+            corrected_done(steps[7], 7, first_turn + 7)
+
+        for n in range(0, 7):
             corrected_done(steps[n], n, first_turn + n)
 
     wait_on(corrected, corr_in)
@@ -462,11 +529,11 @@
 def on_device(initial, estimate, feed_rate, kill_rate):
     dma = pltpu.SemaphoreType.DMA
     vmem = pltpu.VMEM
-    return pl.pallas_call(
+    both = pl.pallas_call(
         kernel,
-        out_shape=(jax.ShapeDtypeStruct(estimate.shape, F32), jax.ShapeDtypeStruct(estimate.shape, F32)),
+        out_shape=jax.ShapeDtypeStruct((2,) + estimate.shape, F32),
         in_specs=[pl.BlockSpec(memory_space=pl.ANY)] * 4,
-        out_specs=[pl.BlockSpec(memory_space=pl.ANY)] * 2,
+        out_specs=pl.BlockSpec(memory_space=pl.ANY),
         scratch_shapes=[
             vmem((FIELDS, 2, 16, 16, 128), F32),
             vmem((TRAIL, 5, 2, 4, 8, 128), F32),
@@ -480,13 +547,14 @@
             vmem((2, 2, 128, 128), F32),
             dma((TRAIL,)), dma((LAST_PACK + 1,)), dma((TRAIL,)), dma((TRAIL,)),
             dma((16,)), dma((4, 2)), dma((SLOTS, 4)), dma((9, 4)),
-            dma, dma, dma, dma, dma,
+            dma, dma, dma, dma, dma, pltpu.SemaphoreType.REGULAR,
         ],
         compiler_params=pltpu.CompilerParams(
             collective_id=0, has_side_effects=True, vmem_limit_bytes=63 * 1024 * 1024
         ),
         name="mgrit_cycle",
     )(initial, estimate, feed_rate, kill_rate)
+    return both[0], both[1]
 
 
 def solution(mesh):

time: 63.9 us -> 58.2 us (0.911)
  Pallas kernels: 60.7 us -> 55 us
    pallas_call x1, Pallas kernels: 60.7 us -> 55 us  [on_device(): pl.pallas_call(kernel, out_shape=jax.ShapeDtypeStruct((2,) + estimate.sha...]
    unnamed x4 -> x0, local copies, waits for them, and re-layouts: 2.42 us -> none
    squeeze x0 -> x1, local copies, waits for them, and re-layouts: none -> 1.86 us  [on_device(): return (both[0], both[1])]
where the time goes in v3:
time: 58.2 us; the launch traced here: 57.5 us
  Pallas kernels  55 us (95%)
  local copies, waits for them, and re-layouts  1.86 us (3%)
  between operations  0.64 us (1%)
    pallas_call x1, Pallas kernels, on_device(): pl.pallas_call(kernel, out_shape=jax.ShapeDtypeStruct((2,) + estimate.sha...  55 us
    squeeze x1, local copies, waits for them, and re-layouts, on_device(): return (both[0], both[1])  1.86 us

profile of v3, /device:TPU:57, one launch (start us, length us, event | category | flops | bytes accessed | tf_op | source)
XLA Modules:
  0.0 57.5 jit_solution(446381523347794675)
XLA Ops:
  0.6 55.0 %mgrit_cycle.1 = f32[2,1,2,2,128,128]{5,4,3,2,1,0:T(8,128)} custom-call(f32[2,2,128,128]{3,2,1,0:T(8,128)} %initial.1, f32[1,2,2,128,128]{4,3,2,1,0:T(8,128)} %estimate.1, f32[2,128,128]{2,1,0:T(8,128)} %feed.1, f32[2,128,128]{2,1,0:T(8,128)} %kill.1), custom_call_target="tpu_custom_call" | custom-call | tf_op jit(solution)/shard_map/mgrit_cycle/pallas_call | solution.py:532
  55.7 1.9 %slice_bitcast_fusion = (f32[1,2,2,128,128]{4,3,2,1,0:T(8,128)}, f32[1,2,2,128,128]{4,3,2,1,0:T(8,128)}) fusion(f32[2,1,2,2,128,128]{5,4,3,2,1,0:T(8,128)} %mgrit_cycle.1), kind=kLoop, calls=%fused_computation | loop fusion | bytes 1048576 | tf_op jit(solution)/shard_map/squeeze | solution.py:557

commit v4 on v3

--- a/solution.py
+++ b/solution.py
@@ -397,6 +397,7 @@
         @pl.when(late_half == 1)
         def _():
             wait_on(block_of(START), block_in.at[START])
+            corrected_put(START, 0, 8)
 
         coarse_step(steps[0], steps[1], DEFECT, 1, 15, True)
         coarse_step(steps[1], steps[2], DEFECT + 1, 2, 14, True)
@@ -414,7 +415,7 @@
 
         @pl.when(late_half == 1)
         def _():
-            for n in range(0, 5):
+            for n in range(1, 5):
                 corrected_put(steps[n], n, first_turn + n)
 
         for n in range(4, 6):

time: 58.2 us -> 57.9 us (level)
  no operation moved by 1% of the time
where the time goes in v4:
time: 57.9 us; the launch traced here: 57.4 us
  Pallas kernels  54.9 us (95%)
  local copies, waits for them, and re-layouts  1.86 us (3%)
  between operations  0.64 us (1%)
    pallas_call x1, Pallas kernels, on_device(): pl.pallas_call(kernel, out_shape=jax.ShapeDtypeStruct((2,) + estimate.sha...  54.9 us
    squeeze x1, local copies, waits for them, and re-layouts, on_device(): return (both[0], both[1])  1.86 us

profile of v4, /device:TPU:57, one launch (start us, length us, event | category | flops | bytes accessed | tf_op | source)
XLA Modules:
  0.0 57.4 jit_solution(1052281135526857431)
XLA Ops:
  0.6 54.9 %mgrit_cycle.1 = f32[2,1,2,2,128,128]{5,4,3,2,1,0:T(8,128)} custom-call(f32[2,2,128,128]{3,2,1,0:T(8,128)} %initial.1, f32[1,2,2,128,128]{4,3,2,1,0:T(8,128)} %estimate.1, f32[2,128,128]{2,1,0:T(8,128)} %feed.1, f32[2,128,128]{2,1,0:T(8,128)} %kill.1), custom_call_target="tpu_custom_call" | custom-call | tf_op jit(solution)/shard_map/mgrit_cycle/pallas_call | solution.py:533
  55.6 1.9 %slice_bitcast_fusion = (f32[1,2,2,128,128]{4,3,2,1,0:T(8,128)}, f32[1,2,2,128,128]{4,3,2,1,0:T(8,128)}) fusion(f32[2,1,2,2,128,128]{5,4,3,2,1,0:T(8,128)} %mgrit_cycle.1), kind=kLoop, calls=%fused_computation | loop fusion | bytes 1048576 | tf_op jit(solution)/shard_map/squeeze | solution.py:558
